TPU v7x, 128 devices: a whole 4x4x4 slice. The times are simulated.
128 devices in a mesh: row: 16 (over z, y_hi, core), col: 8 (over x, y_lo).
Axes of the slice: x: 4, y: 4 (y_hi: 2, y_lo: 2; y = y_hi * 2 + y_lo), z: 4, core: 2. Of those that a mesh axis runs over, the one named last changes fastest.
Arguments:
- roll_hidden: bfloat16 [5376, 4096], P(('row', 'col')), may hold values from -6 to 6
- roll_cotangent: bfloat16 [5376, 4096], P(('row', 'col')), may hold values from -6 to 6
- lengths: int32 [128], P(('row', 'col')), may hold values from 1 to 42, as said below
- owners: int32 [128], P(('row', 'col')), may hold values from 0 to 15, as said below
- prompts: int32 [128], P(('row', 'col')), may hold values from 0 to 15
- rewards: float32 [128], P(('row', 'col')), may hold values from -5 to 5
- gate_weight: bfloat16 [4096, 14784], P('col', 'row'), may hold values from -0.09375 to 0.09375
- up_weight: bfloat16 [4096, 14784], P('col', 'row'), may hold values from -0.09375 to 0.09375
- down_weight: bfloat16 [14784, 4096], P('row', 'col'), may hold values from -0.046875 to 0.046875
Outputs:
- grad_input: bfloat16 [2048, 4096], P('row', 'col')
- grad_gate: bfloat16 [4096, 14784], P('col', 'row')
- grad_up: bfloat16 [4096, 14784], P('col', 'row')
- grad_down: bfloat16 [14784, 4096], P('row', 'col')
Inputs may be any that keep to these rules, and one draw needn't show every extreme that they name: `owners`: each owner value names exactly 8 rows; the lengths of one owner's rows sum to at most 128, and to exactly 128 for some owner in every draw. `lengths`: some row has length 42 in every draw.
All inputs are finite; a program needn't handle non-finite values.
Results may differ from a plain program's by a relative error of at most 0.025.
Values may be sent and summed in bfloat16 or wider, within the bound.
No kernel may reach another device: no remote copies, remote signals or barrier semaphores. Data moves between devices by JAX's collectives and lax.ppermute only.
A program may use at most 128 MiB of HBM per device.

v0:
```python
import jax
import jax.numpy as jnp
from jax import lax
from jax.sharding import PartitionSpec as P

CAPR = 128
spread_floor = 0.7


def in_one_piece(arrays, axis, split_dim, concat_dim, along):
    ends, at = ([], 0)
    for a in arrays[:-1]:
        at += a.shape[along]
        ends.append(at)
    both = jnp.concatenate(arrays, axis=along)
    return tuple(
        jnp.split(
            lax.all_to_all(both, axis, split_axis=split_dim, concat_axis=concat_dim, tiled=True),
            ends,
            axis=along,
        )
    )


def sent_together(arrays, axis, dim, along):
    widths = [a.shape[along] for a in arrays]
    both = jnp.concatenate(arrays, axis=along)
    result = lax.all_gather(both, axis, axis=dim, tiled=True)
    return tuple(jnp.split(result, [sum(widths[:k]) for k in range(1, len(widths))], axis=along))


def cut_along(array, dim, size):
    lengths = array.shape
    tiles = array.reshape(*lengths[:dim], size, lengths[dim] // size, *lengths[dim + 1 :])
    return jnp.moveaxis(tiles, dim, 0)


def sent_and_summed(array, axis, dim):
    size = lax.axis_size(axis)
    tiles = lax.all_to_all(cut_along(array, dim, size), axis, 0, 0, tiled=True)
    return jnp.sum(tiles.astype(jnp.float32), axis=0)


def row_weights(lengths, prompts, rewards, count_prompts):
    onehot = (prompts[:, None] == jnp.arange(count_prompts, dtype=jnp.int32)[None, :]).astype(
        jnp.float32
    )
    counts = jnp.maximum(jnp.sum(onehot, 0), 1.0)
    means = jnp.sum(onehot * rewards[:, None], 0) / counts
    centred = rewards - jnp.sum(onehot * means[None, :], 1)
    spreads = jnp.sqrt(jnp.sum(onehot * (centred * centred)[:, None], 0) / counts)
    divisor = jnp.maximum(jnp.sum(onehot * spreads[None, :], 1), spread_floor)
    return centred / divisor / lengths.astype(jnp.float32)


def row_offsets(lengths, owners):
    count = lengths.shape[0]
    places = jnp.arange(count, dtype=jnp.int32)
    earlier = (owners[None, :] == owners[:, None]) & (places[None, :] < places[:, None])
    return jnp.sum(jnp.where(earlier, lengths[None, :], 0), 1)


def source_index(lengths, owners, offsets, slot_count, capacity, total):
    count = lengths.shape[0]
    slots = jnp.arange(slot_count, dtype=jnp.int32)
    live = slots[None, :] < lengths[:, None]
    target = jnp.where(live, owners[:, None] * capacity + offsets[:, None] + slots[None, :], total)
    flat_source = slots[None, :] * count + jnp.arange(count, dtype=jnp.int32)[:, None]
    empty = jnp.full((total,), slot_count * count, jnp.int32)
    return empty.at[target.reshape(-1)].set(flat_source.reshape(-1), mode="drop")


def per_device(
    roll_hidden,
    roll_cotangent,
    lengths,
    owners,
    prompts,
    rewards,
    gate_weight,
    up_weight,
    down_weight,
):
    row_count = lax.axis_size("row")
    col_count = lax.axis_size("col")
    total_tokens = row_count * CAPR
    count_prompts = row_count * col_count // 8
    slot_count = roll_hidden.shape[0]
    width = roll_hidden.shape[1] // col_count
    local = jnp.stack(
        [
            lengths.astype(jnp.float32),
            owners.astype(jnp.float32),
            prompts.astype(jnp.float32),
            rewards,
        ],
        axis=1,
    )
    table = lax.all_gather(local, ("row", "col"), axis=0, tiled=True)
    all_lengths = table[:, 0].astype(jnp.int32)
    all_owners = table[:, 1].astype(jnp.int32)
    all_prompts = table[:, 2].astype(jnp.int32)
    weights = row_weights(all_lengths, all_prompts, table[:, 3], count_prompts)
    offsets = row_offsets(all_lengths, all_owners)
    mine = lax.dynamic_slice_in_dim(weights, lax.axis_index(("row", "col")), 1, 0)
    live = (jnp.arange(slot_count, dtype=jnp.int32) < lengths[0])[:, None]
    upstream = jnp.where(live, roll_cotangent.astype(jnp.float32) * mine[0], 0.0).astype(
        jnp.bfloat16
    )
    hidden_blocks = roll_hidden.reshape(slot_count, col_count, width)
    upstream_blocks = upstream.reshape(slot_count, col_count, width)
    hidden_cols, upstream_cols = in_one_piece((hidden_blocks, upstream_blocks), "col", 1, 1, 0)
    hidden_all, upstream_all = sent_together((hidden_cols, upstream_cols), "row", 1, 0)
    sources = source_index(all_lengths, all_owners, offsets, slot_count, CAPR, total_tokens)
    packed = jnp.take(hidden_all.reshape(-1, width), sources, axis=0, mode="fill", fill_value=0)
    packed_grad = jnp.take(
        upstream_all.reshape(-1, width), sources, axis=0, mode="fill", fill_value=0
    )
    gate_term = jnp.dot(packed, gate_weight, preferred_element_type=jnp.float32)
    up_term = jnp.dot(packed, up_weight, preferred_element_type=jnp.float32)
    gate, upval = (
        lax.psum(gate_term.astype(jnp.bfloat16), "col").astype(jnp.float32),
        lax.psum(up_term.astype(jnp.bfloat16), "col").astype(jnp.float32),
    )
    sig = jax.nn.sigmoid(gate)
    silu = gate * sig
    hidden = (silu * upval).astype(jnp.bfloat16)
    contract_cols = (((1,), (1,)), ((), ()))
    grad_term = lax.dot_general(
        packed_grad, down_weight, contract_cols, preferred_element_type=jnp.float32
    )
    grad_hidden = lax.psum(grad_term.astype(jnp.bfloat16), "col").astype(jnp.float32)
    grad_gate_act = (grad_hidden * upval * sig * (1.0 + gate * (1.0 - sig))).astype(jnp.bfloat16)
    grad_up_act = (grad_hidden * silu).astype(jnp.bfloat16)
    contract_rows = (((0,), (0,)), ((), ()))
    grad_down = lax.dot_general(
        hidden, packed_grad, contract_rows, preferred_element_type=jnp.float32
    ).astype(jnp.bfloat16)
    grad_gate = lax.dot_general(
        packed, grad_gate_act, contract_rows, preferred_element_type=jnp.float32
    ).astype(jnp.bfloat16)
    grad_up = lax.dot_general(
        packed, grad_up_act, contract_rows, preferred_element_type=jnp.float32
    ).astype(jnp.bfloat16)
    term = lax.dot_general(
        grad_gate_act, gate_weight, contract_cols, preferred_element_type=jnp.float32
    )
    grad_input = sent_and_summed(
        (
            term
            + lax.dot_general(
                grad_up_act, up_weight, contract_cols, preferred_element_type=jnp.float32
            )
        ).astype(jnp.bfloat16),
        "row",
        0,
    )
    return (grad_input.astype(jnp.bfloat16), grad_gate, grad_up, grad_down)


def solution(mesh):
    return jax.shard_map(
        per_device,
        mesh=mesh,
        in_specs=(
            P(("row", "col"), None),
            P(("row", "col"), None),
            P(("row", "col")),
            P(("row", "col")),
            P(("row", "col")),
            P(("row", "col")),
            P("col", "row"),
            P("col", "row"),
            P("row", "col"),
        ),
        out_specs=(P("row", "col"), P("col", "row"), P("col", "row"), P("row", "col")),
        check_vma=False,
    )
```

profile of v0, /device:TPU:4, one launch (start us, length us, event | category | flops | bytes accessed | tf_op | source)
XLA Modules:
  0.0 991.0 jit_solution(10023484400698001869)
XLA Ops:
  10.0 307.3 %all-gather = f32[128,1,4]{2,1,0:T(1,128)S(1)} all-gather(f32[1,1,4]{2,1,0:T(1,128)S(1)} %maximum_bitcast_fusion), channel_id=1, replica_groups=mesh['row'=16,'col'=8] {'row','col'}, dimensions={0}, use_global_device_ids=true | all-gather | bytes 2064 | tf_op jit(solution)/shard_map/all_gather | solution.py:99
  317.3 0.1 convert_reduce_fusion
  317.6 0.1 select_reduce_fusion.2
  317.8 0.6 dynamic_slice.3
  318.4 1.8 select_convert_fusion
  320.2 0.1 copy.31
  320.3 1.1 copy.30
  321.6 0.2 copy.28
  321.8 19.5 %all_to_all.10 = bf16[84,8,512]{2,0,1:T(8,128)(2,1)S(1)} all-to-all(bf16[84,8,512]{2,0,1:T(8,128)(2,1)S(1)} %copy.28), channel_id=1, replica_groups=mesh['row'=16,'col'=8] {'col'}, dimensions={1} | all-to-all | bytes 1376256 | tf_op jit(solution)/shard_map/all_to_all | solution.py:18
  341.3 1.1 copy.29
  342.4 0.1 reshape.149
  342.6 0.2 select_reduce_fusion
  342.8 0.1 add_select_fusion
  342.9 0.2 select_n.47
  343.1 20.4 %scatter_custom_fusion = s32[2048]{0:T(1024)S(1)} fusion(s32[5376]{0:T(1024)S(1)} %fusion.15, s32[5376]{0:T(1024)S(1)} %reshape.149, s32[]{:T(128)} %constant.19.clone.1), kind=kCustom, calls=%fused_computation.47 | custom fusion | bytes 8196 | tf_op jit(solution)/shard_map/scatter | solution.py:70
  363.5 65.8 %all-gather.3.cloned.1.call-done = bf16[84,128,512]{2,1,0:T(8,128)(2,1)} async-done(((bf16[84,8,512]{2,1,0:T(8,128)(2,1)}), bf16[84,128,512]{2,1,0:T(8,128)(2,1)}) %all-gather.3.cloned.1.call-update) | async-done | bytes 11010064 | tf_op jit(solution)/shard_map/all_gather | solution.py:28
  429.3 9.6 fusion.25
  438.9 10.9 %gather_fusion = bf16[2048,512]{1,0:T(8,128)(2,1)S(1)} fusion(bf16[5376,512]{1,0:T(8,128)(2,1)} %bitcast.57, s32[2048]{0:T(1024)S(1)} %fusion.16), kind=kCustom, calls=%fused_computation.clone | custom fusion | bytes 4202496 | tf_op jit(solution)/shard_map/jit(_take)/gather | solution.py:116
  449.8 13.2 %gather_fusion.1 = bf16[2048,512]{1,0:T(8,128)(2,1)} fusion(bf16[5376,512]{1,0:T(8,128)(2,1)} %bitcast.56, s32[2048]{0:T(1024)S(1)} %fusion.16), kind=kCustom, calls=%fused_computation.1.clone | custom fusion | bytes 4202496 | tf_op jit(solution)/shard_map/jit(_take)/gather | solution.py:115
  463.0 5.9 convolution_convert_fusion
  468.9 3.9 convolution_convert_fusion.1
  472.8 3.9 convolution_convert_fusion.2
  476.7 455.9 %all-reduce.3.cloned.1.call-done = (bf16[2048,924]{0,1:T(8,128)(2,1)}, bf16[2048,924]{0,1:T(8,128)(2,1)}, bf16[2048,924]{0,1:T(8,128)(2,1)}) async-done(((bf16[2048,924]{0,1:T(8,128)(2,1)}, bf16[2048,924]{0,1:T(8,128)(2,1)}, bf16[2048,924]{0,1:T(8,128)(2,1)}), (bf16[2048,924]{0,1:T(8,128)(2,1)}, bf16[2048,924]{0,1:T(8,128)(2,1)}, bf16[2048,924]{0,1:T(8,128)(2,1)})) %all-reduce.3.cloned.1.call-update) | async-done | bytes 11354128 | tf_op jit(solution)/shard_map/psum | solution.py:123
  932.6 7.3 fusion
  939.9 3.1 convolution_convert_fusion.3
  943.0 2.4 fusion.26
  945.5 3.9 add_convert_fusion
  949.4 4.5 all-to-all-start.1
  953.9 6.0 convolution_convert_fusion.4
  959.9 3.5 fusion.11
  963.4 19.8 %all-to-all-done.1 = bf16[16,128,512]{2,1,0:T(8,128)(2,1)S(1)} async-done(((bf16[16,128,512]{2,1,0:T(8,128)(2,1)}), bf16[16,128,512]{2,1,0:T(8,128)(2,1)S(1)}, u32[]{:S(2)}, u32[]{:S(2)}) %all-to-all-start.1) | async-done | bytes 2097184 | tf_op jit(solution)/shard_map/all_to_all | solution.py:40
  983.2 1.0 reduce_sum.78
  (47 shorter events, 0.8 us)
Async XLA Ops:
  7.2 455.9 %copy-start = (bf16[512,924]{0,1:T(8,128)(2,1)S(1)}, bf16[512,924]{0,1:T(8,128)(2,1)}, u32[]{:S(2)}) copy-start(bf16[512,924]{0,1:T(8,128)(2,1)} %param.17) | copy-start | bytes 2838532
  7.2 422.2 %all-gather.3.cloned.1.call-start = ((), (), s32[]{:S(2)}) async-start(), calls=%async_computation.2 | async-start | bytes 11698176 | tf_op jit(solution)/shard_map/all_gather | solution.py:28
  342.4 590.2 %all-reduce.3.cloned.1.call-start = ((), (), s32[]{:S(2)}) async-start(), calls=%async_computation.3 | async-start | bytes 22806528 | tf_op jit(solution)/shard_map/psum | solution.py:123
  449.8 23.0 %copy-start.5 = (bf16[2048,512]{1,0:T(8,128)(2,1)}, bf16[2048,512]{1,0:T(8,128)(2,1)S(1)}, u32[]{:S(2)}) copy-start(bf16[2048,512]{1,0:T(8,128)(2,1)S(1)} %gather_fusion) | copy-start | bytes 6291460
  463.0 5.9 copy-start.7
  463.0 5.9 copy-start.10
  468.9 3.9 copy-start.9
  932.6 7.3 copy-start.8
  939.9 3.2 copy-start.4
  943.0 2.4 copy-start.11
  949.4 33.8 %all-to-all-start.1 = ((bf16[16,128,512]{2,1,0:T(8,128)(2,1)}), bf16[16,128,512]{2,1,0:T(8,128)(2,1)S(1)}, u32[]{:S(2)}, u32[]{:S(2)}) async-start(bf16[16,128,512]{2,1,0:T(8,128)(2,1)} %bitcast.58), calls=%async_computation.1 | async-start | bytes 4194304 | tf_op jit(solution)/shard_map/all_to_all | solution.py:40
  953.9 6.0 copy-start.2
  953.9 6.0 copy-start.3
  953.9 6.0 copy-start.6
  959.9 24.2 %copy-start.1 = (bf16[512,924]{0,1:T(8,128)(2,1)S(1)}, bf16[512,924]{0,1:T(8,128)(2,1)}, u32[]{:S(2)}) copy-start(bf16[512,924]{0,1:T(8,128)(2,1)} %param.17) | copy-start | bytes 2838532
Sparse Core Ops, SparseCore 0:
  342.5 86.7 all-gather.2
  476.8 455.7 all-reduce.2
where the time goes:
time: 991 us
  waiting for transfers between devices  542 us (55%)
  blocking collectives  327 us (33%)
  local copies, waits for them, and re-layouts  57.6 us (6%)
  matrix products  32.5 us (3%)
  between operations  17 us (2%)
  other arithmetic  11 us (1%)
    psum x1, waiting for transfers between devices, per_device(): lax.psum(up_term.astype(jnp.bfloat16), 'col').astype(jnp.float32)  456 us
    all_gather x1, blocking collectives, per_device(): table = lax.all_gather(local, ('row', 'col'), axis=0, tiled=True)  307 us
    all_gather x1, waiting for transfers between devices, sent_together(): result = lax.all_gather(both, axis, axis=dim, tiled=True)  65.8 us
    scatter x1, local copies, waits for them, and re-layouts, source_index(): empty.at[target.reshape(-1)].set(flat_source.reshape(-1), mode='drop')  20.4 us
  transfers between devices with their start and end apart: 3, of which 3 were waited for; matrix products, arithmetic and copies ran while one was open for 3% of the time, Pallas kernels for 0%

commit v1 on v0

--- a/solution.py
+++ b/solution.py
@@ -96,7 +96,13 @@
         ],
         axis=1,
     )
-    table = lax.all_gather(local, ("row", "col"), axis=0, tiled=True)
+    work_heads = lambda body: jnp.concatenate(
+        jax.lax.all_to_all(
+            jnp.stack(jax.lax.axis_size(("row", "col")) * [body]), ("row", "col"), 0, 0
+        ),
+        0,
+    )
+    table = work_heads(local)
     all_lengths = table[:, 0].astype(jnp.int32)
     all_owners = table[:, 1].astype(jnp.int32)
     all_prompts = table[:, 2].astype(jnp.int32)

time: 991 us -> 699 us (0.71)
  blocking collectives: 327 us -> 14.9 us
  starting transfers between devices: 4.6 us -> 15.1 us
    all_gather x1 -> x0, blocking collectives: 307 us -> none  [per_device(): table = lax.all_gather(local, ('row', 'col'), axis=0, tiled=True)]
    all_to_all x0 -> x1, starting transfers between devices: none -> 10.5 us  [per_device(): jax.lax.all_to_all(jnp.stack(jax.lax.axis_size(('row', 'col')) * [body]),...]
  transfers between devices with their start and end apart: 3 -> 4, of which waited for: 3 -> 4; matrix products, arithmetic and copies ran while one was open for 3% -> 5% of each run, Pallas kernels for 0% -> 0%
where the time goes in v1:
time: 699 us
  waiting for transfers between devices  550 us (79%)
  local copies, waits for them, and re-layouts  58.3 us (8%)
  matrix products  32.5 us (5%)
  between operations  17 us (2%)
  starting transfers between devices  15.1 us (2%)
  blocking collectives  14.9 us (2%)
  other arithmetic  11 us (2%)
    psum x1, waiting for transfers between devices, per_device(): lax.psum(up_term.astype(jnp.bfloat16), 'col').astype(jnp.float32)  456 us
    all_gather x1, waiting for transfers between devices, sent_together(): result = lax.all_gather(both, axis, axis=dim, tiled=True)  67.7 us
    scatter x1, local copies, waits for them, and re-layouts, source_index(): empty.at[target.reshape(-1)].set(flat_source.reshape(-1), mode='drop')  20.4 us
    all_to_all x1, waiting for transfers between devices, sent_and_summed(): tiles = lax.all_to_all(cut_along(array, dim, size), axis, 0, 0, tiled=True)  19.8 us
    all_to_all x1, blocking collectives, in_one_piece(): lax.all_to_all(both, axis, split_axis=split_dim, concat_axis=concat_dim,...  14.9 us
  transfers between devices with their start and end apart: 4, of which 4 were waited for; matrix products, arithmetic and copies ran while one was open for 5% of the time, Pallas kernels for 0%

profile of v1, /device:TPU:4, one launch (start us, length us, event | category | flops | bytes accessed | tf_op | source)
XLA Modules:
  0.0 698.9 jit_solution(8992971033206636793)
XLA Ops:
  9.9 0.7 stack.20
  10.6 10.5 %all-to-all-start = ((f32[128,1,4]{2,1,0:T(1,128)}), f32[128,1,4]{2,1,0:T(1,128)S(1)}, u32[]{:S(2)}, u32[]{:S(2)}) async-start(f32[128,1,4]{2,1,0:T(1,128)} %stack.20), calls=%async_computation | async-start | bytes 131072 | tf_op jit(solution)/shard_map/all_to_all | solution.py:100
  21.2 1.1 copy.26
  22.3 6.7 all-to-all-done
  29.1 0.1 convert_reduce_fusion
  29.6 0.6 dynamic_slice.3
  30.2 1.8 select_convert_fusion
  32.0 0.1 copy.27
  32.2 0.2 copy.24
  32.4 14.9 %all_to_all.15 = bf16[84,8,512]{2,0,1:T(8,128)(2,1)S(1)} all-to-all(bf16[84,8,512]{2,0,1:T(8,128)(2,1)S(1)} %copy.24), channel_id=1, replica_groups=mesh['row'=16,'col'=8] {'col'}, dimensions={1} | all-to-all | bytes 1376256 | tf_op jit(solution)/shard_map/all_to_all | solution.py:18
  47.3 1.1 copy.25
  48.5 0.1 reshape.156
  48.6 0.2 select_reduce_fusion
  48.9 0.2 select_n.47
  49.1 20.4 %scatter_custom_fusion = s32[2048]{0:T(1024)S(1)} fusion(s32[5376]{0:T(1024)S(1)} %fusion.15, s32[5376]{0:T(1024)S(1)} %reshape.156, s32[]{:T(128)} %constant.19.clone.1), kind=kCustom, calls=%fused_computation.47 | custom fusion | bytes 8196 | tf_op jit(solution)/shard_map/scatter | solution.py:70
  69.5 67.7 %all-gather.2.cloned.1.call-done = bf16[84,128,512]{2,1,0:T(8,128)(2,1)} async-done(((bf16[84,8,512]{2,1,0:T(8,128)(2,1)}), bf16[84,128,512]{2,1,0:T(8,128)(2,1)}) %all-gather.2.cloned.1.call-update) | async-done | bytes 11010064 | tf_op jit(solution)/shard_map/all_gather | solution.py:28
  137.2 9.6 %fusion.25 = (bf16[42,128,512]{2,1,0:T(8,128)(2,1)}, bf16[42,128,512]{2,1,0:T(8,128)(2,1)}) fusion(bf16[84,128,512]{2,1,0:T(8,128)(2,1)} %all-gather.2.cloned.1.call-done), kind=kLoop, calls=%fused_computation.67 | loop fusion | bytes 22020096 | tf_op jit(solution)/shard_map/split | solution.py:29
  146.8 10.9 %gather_fusion = bf16[2048,512]{1,0:T(8,128)(2,1)S(1)} fusion(bf16[5376,512]{1,0:T(8,128)(2,1)} %bitcast.57, s32[2048]{0:T(1024)S(1)} %fusion.16), kind=kCustom, calls=%fused_computation.clone | custom fusion | bytes 4202496 | tf_op jit(solution)/shard_map/jit(_take)/gather | solution.py:122
  157.7 13.3 %gather_fusion.1 = bf16[2048,512]{1,0:T(8,128)(2,1)} fusion(bf16[5376,512]{1,0:T(8,128)(2,1)} %bitcast.56, s32[2048]{0:T(1024)S(1)} %fusion.16), kind=kCustom, calls=%fused_computation.1.clone | custom fusion | bytes 4202496 | tf_op jit(solution)/shard_map/jit(_take)/gather | solution.py:121
  171.0 5.9 convolution_convert_fusion
  176.9 3.9 convolution_convert_fusion.1
  180.7 3.8 convolution_convert_fusion.2
  184.6 455.9 %all-reduce.3.cloned.1.call-done = (bf16[2048,924]{0,1:T(8,128)(2,1)}, bf16[2048,924]{0,1:T(8,128)(2,1)}, bf16[2048,924]{0,1:T(8,128)(2,1)}) async-done(((bf16[2048,924]{0,1:T(8,128)(2,1)}, bf16[2048,924]{0,1:T(8,128)(2,1)}, bf16[2048,924]{0,1:T(8,128)(2,1)}), (bf16[2048,924]{0,1:T(8,128)(2,1)}, bf16[2048,924]{0,1:T(8,128)(2,1)}, bf16[2048,924]{0,1:T(8,128)(2,1)})) %all-reduce.3.cloned.1.call-update) | async-done | bytes 11354128 | tf_op jit(solution)/shard_map/psum | solution.py:129
  640.5 7.3 %fusion = (bf16[2048,924]{0,1:T(8,128)(2,1)S(1)}, bf16[2048,924]{0,1:T(8,128)(2,1)S(1)}) fusion(bf16[2048,924]{0,1:T(8,128)(2,1)} %get-tuple-element.8, bf16[2048,924]{0,1:T(8,128)(2,1)} %get-tuple-element.9, bf16[2048,924]{0,1:T(8,128)(2,1)} %get-tuple-element.7), kind=kLoop, calls=%fused_computation.9 | loop fusion | flops 30277632 | bytes 18923520 | tf_op jit(solution)/shard_map/convert_element_type | solution.py:140
  647.8 3.1 convolution_convert_fusion.3
  650.9 2.4 fusion.26
  653.4 3.9 add_convert_fusion
  657.2 4.5 all-to-all-start.2
  661.8 6.0 convolution_convert_fusion.4
  667.8 3.5 fusion.11
  671.3 19.8 %all-to-all-done.2 = bf16[16,128,512]{2,1,0:T(8,128)(2,1)S(1)} async-done(((bf16[16,128,512]{2,1,0:T(8,128)(2,1)}), bf16[16,128,512]{2,1,0:T(8,128)(2,1)S(1)}, u32[]{:S(2)}, u32[]{:S(2)}) %all-to-all-start.2) | async-done | bytes 2097184 | tf_op jit(solution)/shard_map/all_to_all | solution.py:40
  691.1 1.0 reduce_sum.78
  (49 shorter events, 1.0 us)
Async XLA Ops:
  7.2 163.8 %copy-start = (bf16[512,924]{0,1:T(8,128)(2,1)S(1)}, bf16[512,924]{0,1:T(8,128)(2,1)}, u32[]{:S(2)}) copy-start(bf16[512,924]{0,1:T(8,128)(2,1)} %param.17) | copy-start | bytes 2838532
  10.6 18.5 %all-to-all-start = ((f32[128,1,4]{2,1,0:T(1,128)}), f32[128,1,4]{2,1,0:T(1,128)S(1)}, u32[]{:S(2)}, u32[]{:S(2)}) async-start(f32[128,1,4]{2,1,0:T(1,128)} %stack.20), calls=%async_computation | async-start | bytes 131072 | tf_op jit(solution)/shard_map/all_to_all | solution.py:100
  21.1 116.1 %all-gather.2.cloned.1.call-start = ((), (), s32[]{:S(2)}) async-start(), calls=%async_computation.3 | async-start | bytes 11698176 | tf_op jit(solution)/shard_map/all_gather | solution.py:28
  48.4 592.1 %all-reduce.3.cloned.1.call-start = ((), (), s32[]{:S(2)}) async-start(), calls=%async_computation.4 | async-start | bytes 22806528 | tf_op jit(solution)/shard_map/psum | solution.py:129
  157.7 23.1 %copy-start.5 = (bf16[2048,512]{1,0:T(8,128)(2,1)}, bf16[2048,512]{1,0:T(8,128)(2,1)S(1)}, u32[]{:S(2)}) copy-start(bf16[2048,512]{1,0:T(8,128)(2,1)S(1)} %gather_fusion) | copy-start | bytes 6291460
  171.0 5.9 copy-start.7
  171.0 5.9 copy-start.10
  176.9 3.9 copy-start.9
  640.5 7.3 %copy-start.8 = (bf16[2048,512]{1,0:T(8,128)(2,1)S(1)}, bf16[2048,512]{1,0:T(8,128)(2,1)}, u32[]{:S(2)}) copy-start(bf16[2048,512]{1,0:T(8,128)(2,1)} %gather_fusion.1) | copy-start | bytes 6291460
  647.8 3.2 copy-start.4
  650.9 2.4 copy-start.11
  657.2 33.9 %all-to-all-start.2 = ((bf16[16,128,512]{2,1,0:T(8,128)(2,1)}), bf16[16,128,512]{2,1,0:T(8,128)(2,1)S(1)}, u32[]{:S(2)}, u32[]{:S(2)}) async-start(bf16[16,128,512]{2,1,0:T(8,128)(2,1)} %bitcast.58), calls=%async_computation.2 | async-start | bytes 4194304 | tf_op jit(solution)/shard_map/all_to_all | solution.py:40
  661.8 6.0 copy-start.2
  661.8 6.0 copy-start.3
  661.8 6.0 copy-start.6
  667.8 24.2 %copy-start.1 = (bf16[512,924]{0,1:T(8,128)(2,1)S(1)}, bf16[512,924]{0,1:T(8,128)(2,1)}, u32[]{:S(2)}) copy-start(bf16[512,924]{0,1:T(8,128)(2,1)} %param.17) | copy-start | bytes 2838532
Sparse Core Ops, SparseCore 0:
  48.5 88.6 all-gather.1
  184.7 455.7 all-reduce.2
